TPU v7x, 128 devices: a whole 4x4x4 slice. The times are simulated.
128 devices in a mesh: row: 4 (over z), col: 8 (over y, core), cuts: 4 (over x).
Axes of the slice: x: 4, y: 4, z: 4, core: 2. Of those that a mesh axis runs over, the one named last changes fastest.
Arguments:
- t_amp: bfloat16 [3072, 32768], P('row', ('col', 'cuts')), may hold values from -1 to 1
- v_int: bfloat16 [3072, 32768], P('row', ('col', 'cuts')), may hold values from -0.03125 to 0.03125
- block_map: int32 [48, 512], P('row', ('col', 'cuts')), may hold values 0 or 1
Outputs:
- residual: float32 [3072, 32768], P('row', ('col', 'cuts'))
Inputs may be any that keep to these rules, and one draw needn't show every extreme that they name: `block_map`: 0 or 1 for each pair of symmetry blocks.
All inputs are finite; a program needn't handle non-finite values.
Results may differ from a plain program's by a relative error of at most 0.0029.
Values may be sent and summed in bfloat16 or wider, within the bound.
A program may use at most 128 MiB of HBM per device.

v0:
```python
import jax
import jax.numpy as jnp
from jax import lax
from jax.sharding import PartitionSpec as P


def apply_map(values, block_map):
    row_blocks, col_blocks = block_map.shape
    shaped = values.reshape(
        row_blocks, values.shape[0] // row_blocks, col_blocks, values.shape[1] // col_blocks
    )
    weights = block_map.astype(values.dtype)[:, None, :, None]
    return (shaped * weights).reshape(values.shape)


def per_device(t_amp, v_int, block_map):
    masked_t = apply_map(t_amp, block_map)
    masked_v = apply_map(v_int, block_map)
    partial_value = lax.dot_general(
        masked_t,
        lax.all_gather(masked_v, "row", axis=0, tiled=True),
        (((1,), (1,)), ((), ())),
        preferred_element_type=jnp.float32,
    )
    w_pair = lax.psum(partial_value, ("col", "cuts")).astype(jnp.bfloat16)
    result = jnp.dot(
        w_pair,
        lax.all_gather(masked_t, "row", axis=0, tiled=True),
        preferred_element_type=jnp.float32,
    )
    return apply_map(result, block_map)


def solution(mesh):
    placed = (P("row", ("col", "cuts")), P("row", ("col", "cuts")), P("row", ("col", "cuts")))
    return jax.shard_map(
        per_device, mesh=mesh, in_specs=placed, out_specs=P("row", ("col", "cuts")), check_vma=False
    )
```

profile of v0, /device:TPU:1, one launch (start us, length us, event | category | flops | bytes accessed | tf_op | source)
XLA Modules:
  0.0 323.3 jit_solution(5752071568704120806)
XLA Ops:
  6.5 0.0 all-gather.3.cloned.1.call-start
  6.5 0.8 fusion.6
  7.3 0.5 mul.29
  7.8 3.2 mul.30
  10.9 4.3 %fusion.5 = (bf16[768,1024]{1,0:T(8,128)(2,1)}, bf16[768,1024]{1,0:T(8,128)(2,1)}) fusion(bf16[768,1024]{1,0:T(8,128)(2,1)} %param.4, bf16[768,1024]{1,0:T(8,128)(2,1)} %mul.30, bf16[768,1024]{1,0:T(8,128)(2,1)} %param.3), kind=kLoop, calls=%fused_computation.3 | loop fusion | flops 1572864 | bytes 7864320 | tf_op jit(solution)/shard_map/mul | solution.py:13
  15.2 0.0 all-gather.3.cloned.1.call-update
  15.3 0.0 all-gather.5.cloned.1.call-start
  15.3 0.7 all-gather.5.cloned.1.call-update
  16.0 3.1 mul.33
  19.2 0.0 copy-start
  19.2 6.4 %mul.34 = f32[768,1024]{1,0:T(8,128)} reshape(f32[12,64,16,64]{3,2,1,0:T(8,128)} %mul.33) | data formatting | bytes 6291456 | tf_op jit(solution)/shard_map/mul | solution.py:13
  25.6 58.9 %all-gather.3.cloned.1.call-done = bf16[3072,1024]{1,0:T(8,128)(2,1)} async-done(((bf16[768,1024]{1,0:T(8,128)(2,1)}), bf16[3072,1024]{1,0:T(8,128)(2,1)}) %all-gather.3.cloned.1.call-update) | async-done | bytes 6291472 | tf_op jit(solution)/shard_map/all_gather | solution.py:21
  84.5 0.0 copy-done
  84.5 10.2 %fusion.7 = f32[768,3072]{1,0:T(8,128)} fusion(bf16[768,1024]{1,0:T(8,128)(2,1)S(1)} %copy-done, bf16[3072,1024]{1,0:T(8,128)(2,1)} %all-gather.3.cloned.1.call-done), kind=kOutput, calls=%fused_computation.5 | convolution fusion | flops 4831838208 | bytes 17301504 | tf_op jit(solution)/shard_map/dot_general | solution.py:19
  94.8 0.0 copy-start.1
  94.8 212.0 %all-reduce.1 = bf16[768,3072]{1,0:T(8,128)(2,1)} all-reduce(f32[768,3072]{1,0:T(8,128)} %fusion.7), channel_id=1, replica_groups=mesh['row'=4,'col'=8,'cuts'=4] {'col','cuts'}, use_global_device_ids=true, to_apply=%region_0.0 | all-reduce | flops 2359296 | bytes 14155776 | tf_op jit(solution)/shard_map/psum | solution.py:25
  306.8 0.0 all-gather.5.cloned.1.call-done
  306.8 0.0 copy-done.1
  306.8 9.6 %fusion.2 = f32[768,1024]{1,0:T(8,128)} fusion(f32[768,1024]{1,0:T(8,128)S(1)} %copy-done.1, bf16[3072,1024]{1,0:T(8,128)(2,1)} %all-gather.5.cloned.1.call-done, bf16[768,3072]{1,0:T(8,128)(2,1)} %all-reduce.1), kind=kOutput, calls=%fused_computation.2 | convolution fusion | flops 4832624640 | bytes 17301504 | tf_op jit(solution)/shard_map/dot_general | solution.py:26
Async XLA Ops:
  6.5 78.0 %all-gather.3.cloned.1.call-start = ((), (), s32[]{:S(2)}) async-start(), calls=%async_computation | async-start | bytes 7864320 | tf_op jit(solution)/shard_map/all_gather | solution.py:21
  15.3 291.5 %all-gather.5.cloned.1.call-start = ((), (), s32[]{:S(2)}) async-start(), calls=%async_computation.1 | async-start | bytes 7864320 | tf_op jit(solution)/shard_map/all_gather | solution.py:28
  19.2 65.4 %copy-start = (bf16[768,1024]{1,0:T(8,128)(2,1)S(1)}, bf16[768,1024]{1,0:T(8,128)(2,1)}, u32[]{:S(2)}) copy-start(bf16[768,1024]{1,0:T(8,128)(2,1)} %get-tuple-element.6) | copy-start | bytes 4718596
  94.8 212.0 %copy-start.1 = (f32[768,1024]{1,0:T(8,128)S(1)}, f32[768,1024]{1,0:T(8,128)}, u32[]{:S(2)}) copy-start(f32[768,1024]{1,0:T(8,128)} %mul.34) | copy-start | bytes 9437188
Sparse Core Ops, SparseCore 0:
  15.4 69.0 all-gather.2
  86.2 66.4 all-gather.4
where the time goes:
time: 326 us; the launch traced here: 323 us
  blocking collectives  212 us (65%)
  waiting for transfers between devices  59.7 us (18%)
  matrix products  19.9 us (6%)
  between operations  13.4 us (4%)
  local copies, waits for them, and re-layouts  13.2 us (4%)
  other arithmetic  5.07 us (2%)
    psum x1, blocking collectives, per_device(): w_pair = lax.psum(partial_value, ('col', 'cuts')).astype(jnp.bfloat16)  212 us
    all_gather x1, waiting for transfers between devices, per_device(): lax.all_gather(masked_v, 'row', axis=0, tiled=True)  58.9 us
    mul x4, local copies, waits for them, and re-layouts, apply_map(): return (shaped * weights).reshape(values.shape)  13.2 us
    dot_general x1, matrix products, per_device(): lax.dot_general(masked_t, lax.all_gather(masked_v, 'row', axis=0, tiled=T...  10.2 us
    dot_general x1, matrix products, per_device(): jnp.dot(w_pair, lax.all_gather(masked_t, 'row', axis=0, tiled=True), pref...  9.64 us
  transfers between devices with their start and end apart: 2, of which 1 were waited for; matrix products, arithmetic and copies ran while one was open for 6% of the time, Pallas kernels for 0%

commit v1 on v0

v1 whole, which is shorter than its diff:
```python
import functools

import jax
import jax.numpy as jnp
from jax import lax
from jax.experimental import pallas as pl
from jax.experimental.pallas import tpu as pltpu
from jax.sharding import PartitionSpec as P

MESH = pl.DeviceIdType.MESH
CH = 256
UN = 128
NT = (((1,), (1,)), ((), ()))


def kernel(ny, nx, t_ref, v_ref, m_ref, out_ref, tall, mv, mask, part, crecv, s1, r1, s2, r2, wp, wg, acc,
           ts, tr, cs, cr, as_, ar, bs, br, zs, zr, g1s, g1r, g2s, g2r, g3s, g3r):
    rows, cols = t_ref.shape
    half = cols // 2
    nj = rows // CH
    nu = rows // UN
    vh = rows // 2
    z = lax.axis_index("row")
    col = lax.axis_index("col")
    x = lax.axis_index("cuts")
    y = lax.div(col, 2)
    h = lax.rem(col, 2)

    def dev(dz=0, dy=0, dx=0, flip=False):
        hh = 1 - h if flip else h
        return (lax.rem(z + dz, 4), 2 * lax.rem(y + dy, ny) + hh, lax.rem(x + dx, nx))

    partners = [dev(dz=d) for d in (1, 2, 3)] + [dev(flip=True)]
    partners += [dev(dy=d) for d in range(1, ny)] + [dev(dx=d) for d in range(1, nx)]
    barrier = pltpu.get_barrier_semaphore()
    for p in partners:
        pl.semaphore_signal(barrier, inc=1, device_id=p, device_id_type=MESH)

    br_, bc_ = m_ref.shape
    e1 = (lax.broadcasted_iota(jnp.int32, (rows, br_), 0) // 64
          == lax.broadcasted_iota(jnp.int32, (rows, br_), 1)).astype(jnp.bfloat16)
    e2 = (lax.broadcasted_iota(jnp.int32, (bc_, cols), 1) // 64
          == lax.broadcasted_iota(jnp.int32, (bc_, cols), 0)).astype(jnp.bfloat16)
    rm = jnp.dot(e1, m_ref[...], preferred_element_type=jnp.float32).astype(jnp.bfloat16)
    mask[...] = jnp.dot(rm, e2, preferred_element_type=jnp.float32).astype(jnp.bfloat16)
    tall[0] = t_ref[...] * mask[...]
    pl.semaphore_wait(barrier, len(partners))

    def remote(src, dst, ss, rs, to):
        return pltpu.make_async_remote_copy(
            src_ref=src, dst_ref=dst, send_sem=ss, recv_sem=rs, device_id=to, device_id_type=MESH)

    copies = {}
    sent, got = set(), set()

    def start(key, *args):
        copies[key] = remote(*args)
        copies[key].start()

    def wait_send(key):
        if key not in sent:
            sent.add(key)
            copies[key].wait_send()

    def wait_recv(key):
        if key not in got:
            got.add(key)
            copies[key].wait_recv()

    def own(u):
        rs = pl.ds(u * UN, UN)
        if u >= 2:
            wait_send(("t", 0, u - 2))
            wait_send(("t", 1, u - 2))
        start(("t", 0, u), tall.at[0, rs], tall.at[1, rs], ts.at[0, u], tr.at[0, u], dev(dz=1))
        start(("t", 1, u), tall.at[0, rs], tall.at[2, rs], ts.at[1, u], tr.at[1, u], dev(dz=3))

    def fwd(u):
        rs = pl.ds(u * UN, UN)
        for d in (0, 1):
            wait_recv(("t", d, u))
            if u >= 2:
                wait_send(("t", 2 + d, u - 2))
        start(("t", 2, u), tall.at[1, rs, pl.ds(0, half)], tall.at[3, rs, pl.ds(0, half)],
              ts.at[2, u], tr.at[2, u], dev(dz=1))
        start(("t", 3, u), tall.at[2, rs, pl.ds(half, half)], tall.at[3, rs, pl.ds(half, half)],
              ts.at[3, u], tr.at[3, u], dev(dz=3))

    def arrived(r, j):
        for u in range(j * CH // UN, (j + 1) * CH // UN):
            for d in {0: (), 1: (0,), 2: (1,), 3: (2, 3)}[r]:
                wait_recv(("t", d, u))

    order = [(0, j) for j in range(nj)] + [(r, j) for j in range(nj) for r in (1, 2)] + [(3, j) for j in range(nj)]
    index = {c: i for i, c in enumerate(order)}

    def axes(i):
        if i % 2 == 0:
            return y, ny, lambda d: dev(dy=d), x, nx, lambda d: dev(dx=d)
        return x, nx, lambda d: dev(dx=d), y, ny, lambda d: dev(dy=d)

    def gemm1(q):
        r, j = order[q]
        arrived(r, j)
        p = lax.dot_general(tall[r, j * CH:(j + 1) * CH], mv[...], NT, preferred_element_type=jnp.float32)
        part[q, 0] = p[:, :vh]
        part[q, 1] = p[:, vh:]
        start(("c", q), part.at[q, 1 - h], crecv.at[q], cs.at[q], cr.at[q], dev(flip=True))

    def scatter1(q):
        a, na, to, *_ = axes(q)
        g = CH // na
        wait_recv(("c", q))
        full = part[q, h] + crecv[q]
        s1[q] = full.astype(jnp.bfloat16)
        crecv[q] = full
        for d in range(1, na):
            start(("a", q, d), s1.at[q, pl.ds(pl.multiple_of(lax.rem(a + d, na) * g, g), g)], r1.at[q, d - 1],
                  as_.at[q, d - 1], ar.at[q, d - 1], to(d))

    def scatter2(q):
        a, na, _, b, nb, to = axes(q)
        g = CH // na
        k = g // nb
        total = crecv[q, pl.ds(pl.multiple_of(a * g, g), g)]
        for d in range(1, na):
            wait_recv(("a", q, d))
            total = total + r1[q, d - 1].astype(jnp.float32)
        s2[q] = total
        for d in range(1, nb):
            start(("b", q, d), s2.at[q, pl.ds(pl.multiple_of(lax.rem(b + d, nb) * k, k), k)], r2.at[q, d - 1],
                  bs.at[q, d - 1], br.at[q, d - 1], to(d))

    def piece(q):
        a, na, _, b, nb, _ = axes(q)
        g = CH // na
        k = g // nb
        return pl.ds(pl.multiple_of(a * g + b * k, k), k)

    def finish(q):
        r, j = order[q]
        a, na, _, b, nb, _ = axes(q)
        k = CH // na // nb
        total = s2[q, pl.ds(pl.multiple_of(b * k, k), k)]
        for d in range(1, nb):
            wait_recv(("b", q, d))
            total = total + r2[q, d - 1]
        w = total.astype(jnp.bfloat16)
        if r == 0:
            wg[q, h, piece(q)] = w
            gather1(q)
        else:
            wp[q] = w
            start(("z", q), wp.at[q], wg.at[q, h, piece(q)], zs.at[q], zr.at[q], dev(dz={1: 3, 2: 1, 3: 2}[r]))

    def gather1(q):
        _, _, _, b, nb, to = axes(q)
        if order[q][0] != 0:
            wait_recv(("z", q))
        mine = wg.at[q, h, piece(q)]
        for d in range(1, nb):
            start(("g", q, d), mine, mine, g1s.at[q, d - 1], g1r.at[q, d - 1], to(d))

    def gather2(q):
        a, na, to, _, nb, _ = axes(q)
        g = CH // na
        for d in range(1, nb):
            wait_recv(("g", q, d))
        mine = wg.at[q, h, pl.ds(pl.multiple_of(a * g, g), g)]
        for d in range(1, na):
            start(("h", q, d), mine, mine, g2s.at[q, d - 1], g2r.at[q, d - 1], to(d))

    def gather3(q):
        _, na, *_ = axes(q)
        for d in range(1, na):
            wait_recv(("h", q, d))
        start(("i", q), wg.at[q, h], wg.at[q, h], g3s.at[q], g3r.at[q], dev(flip=True))

    def gemm2(q):
        r, j = order[q]
        slot = {0: 0, 1: 2, 2: 1, 3: 3}[r]
        for jj in range(nj):
            arrived(slot, jj)
        wait_recv(("i", q))
        w = jnp.concatenate([wg[q, 0], wg[q, 1]], axis=1)
        p = jnp.dot(w, tall[slot], preferred_element_type=jnp.float32)
        js = slice(j * CH, (j + 1) * CH)
        if r == 0:
            acc[js] = p
        elif r < 3:
            acc[js] = acc[js] + p
        else:
            out_ref[js] = (acc[js] + p) * mask[js].astype(jnp.float32)

    def prepare():
        mv[...] = v_ref[...] * mask[...]

    events = []

    def at(t, f, *args):
        events.append((t, len(events), f, args))

    unit = 5.3
    for u in range(nu):
        at(max(0.0, unit * (u - 1)), own, u)
        at(unit * nu + 0.5 * unit * (u - 1), fwd, u)
    at(0.1, prepare)
    for q, (r, j) in enumerate(order):
        t = {0: 0.2 + 0.8 * j, 1: 2 * unit * (j + 1) + 1, 2: 2 * unit * (j + 1) + 1.8,
             3: nu * unit + unit * (j + 1) + 2}[r]
        at(t, gemm1, q)
        at(t + 2.6, scatter1, q)
        at(t + 5.6, scatter2, q)
        at(t + 7.6, finish, q)
        if r == 0:
            t -= 2
        else:
            at(t + 9.6, gather1, q)
        at(t + 11.6, gather2, q)
        at(t + 14.6, gather3, q)
        t += 16.2
        if r in (1, 2):
            t = max(t, unit * nu + 3)
        at(t, gemm2, q)
    for _, _, f, args in sorted(events, key=lambda e: e[:2]):
        f(*args)
    for key in copies:
        wait_send(key)


def per_device(t_amp, v_int, block_map, ny, nx):
    rows, cols = t_amp.shape
    nq = 4 * rows // CH
    vh = rows // 2
    k = CH // ny // nx
    bf, f32 = jnp.bfloat16, jnp.float32
    na = max(ny, nx)
    g = CH // min(ny, nx)
    dma = pltpu.SemaphoreType.DMA
    m = jnp.pad(block_map.astype(bf), ((0, 16 - block_map.shape[0]), (0, 128 - block_map.shape[1])))
    vmem = pl.BlockSpec(memory_space=pltpu.VMEM)
    return pl.pallas_call(
        functools.partial(kernel, ny, nx),
        out_shape=jax.ShapeDtypeStruct((rows, cols), f32),
        in_specs=[vmem] * 3,
        out_specs=vmem,
        scratch_shapes=[
            pltpu.VMEM((4, rows, cols), bf),
            pltpu.VMEM((rows, cols), bf),
            pltpu.VMEM((rows, cols), bf),
            pltpu.VMEM((nq, 2, CH, vh), f32),
            pltpu.VMEM((nq, CH, vh), f32),
            pltpu.VMEM((nq, CH, vh), bf),
            pltpu.VMEM((nq, na - 1, g, vh), bf),
            pltpu.VMEM((nq, g, vh), f32),
            pltpu.VMEM((nq, na - 1, k, vh), f32),
            pltpu.VMEM((nq, k, vh), bf),
            pltpu.VMEM((nq, 2, CH, vh), bf),
            pltpu.VMEM((rows, cols), f32),
            dma((4, rows // UN)), dma((4, rows // UN)),
            dma((nq,)), dma((nq,)),
            dma((nq, na - 1)), dma((nq, na - 1)),
            dma((nq, na - 1)), dma((nq, na - 1)),
            dma((nq,)), dma((nq,)),
            dma((nq, na - 1)), dma((nq, na - 1)),
            dma((nq, na - 1)), dma((nq, na - 1)),
            dma((nq,)), dma((nq,)),
        ],
        compiler_params=pltpu.CompilerParams(
            collective_id=0, has_side_effects=True, vmem_limit_bytes=60 * 2**20),
        cost_estimate=pl.CostEstimate(flops=4 * rows * 4 * rows * cols, bytes_accessed=10 * rows * cols, transcendentals=0),
    )(t_amp, v_int, m)


def solution(mesh):
    spec = P("row", ("col", "cuts"))
    body = functools.partial(per_device, ny=mesh.shape["col"] // 2, nx=mesh.shape["cuts"])
    return jax.shard_map(body, mesh=mesh, in_specs=(spec,) * 3, out_specs=spec, check_vma=False)
```

time: 326 us -> 126 us (0.39)
  blocking collectives: 212 us -> 0 us
  Pallas kernels: 0 us -> 120 us
  waiting for transfers between devices: 59.7 us -> 0 us
  matrix products: 19.9 us -> 0 us
  between operations: 13.4 us -> 0.01 us
  local copies, waits for them, and re-layouts: 13.2 us -> 4.57 us
  other arithmetic: 5.07 us -> 0.7 us
    psum x1 -> x0, blocking collectives: 212 us -> none  [per_device(): w_pair = lax.psum(partial_value, ('col', 'cuts')).astype(jnp.bfloat16)]
    pallas_call x0 -> x1, Pallas kernels: none -> 120 us  [per_device(): pl.pallas_call(functools.partial(kernel, ny, nx), out_shape=jax.ShapeDtyp...]
    all_gather x2 -> x0, waiting for transfers between devices: 58.9 us -> none  [the longest x1 58.9 us: per_device(): lax.all_gather(masked_v, 'row', axis=0, tiled=True)]
    dot_general x2 -> x0, matrix products: 19.9 us -> none  [the longest x1 10.2 us: per_device(): lax.dot_general(masked_t, lax.all_gather(masked_v, 'row', axis=0, tiled=T...]
    mul x4 -> x0, local copies, waits for them, and re-layouts: 13.2 us -> none  [apply_map(): return (shaped * weights).reshape(values.shape)]
    mul x1 -> x0, other arithmetic: 4.3 us -> none  [apply_map(): return (shaped * weights).reshape(values.shape)]
    unnamed x4 -> x1, local copies, waits for them, and re-layouts: 0.01 us -> 3.97 us
  transfers between devices with their start and end apart: 2 -> 0, of which waited for: 1 -> 0; matrix products, arithmetic and copies ran while one was open for 6% -> 0% of each run, Pallas kernels for 0% -> 0%
where the time goes in v1:
time: 126 us
  Pallas kernels  120 us (95%)
  local copies, waits for them, and re-layouts  4.57 us (4%)
    pallas_call x1, Pallas kernels, per_device(): pl.pallas_call(functools.partial(kernel, ny, nx), out_shape=jax.ShapeDtyp...  120 us
    unnamed x1, local copies, waits for them, and re-layouts  3.97 us

profile of v1, /device:TPU:1, one launch (start us, length us, event | category | flops | bytes accessed | tf_op | source)
XLA Modules:
  0.0 125.5 jit_solution(12523741338850306477)
XLA Ops:
  0.0 0.7 convert_element_type.5
  0.7 0.6 pad.4.m_ref
  1.3 120.3 %shard_map.37 = f32[768,1024]{1,0:T(8,128)} custom-call(bf16[768,1024]{1,0:T(8,128)(2,1)} %t_ref.1, bf16[768,1024]{1,0:T(8,128)(2,1)} %v_ref.1, bf16[16,128]{1,0:T(8,128)(2,1)} %pad.4.m_ref), custom_call_target="tpu_custom_call" | custom-call | flops 9663676416 | bytes 7864320 | tf_op jit(solution)/shard_map/pallas_call | solution.py:242
  121.6 4.0 %copy.5 = f32[768,1024]{1,0:T(8,128)} copy(f32[768,1024]{1,0:T(8,128)} %shard_map.37) | data formatting | bytes 6291456

commit v2 on v1

v2 whole, which is shorter than its diff:
```python
import functools

import jax
import jax.numpy as jnp
from jax import lax
from jax.experimental import pallas as pl
from jax.experimental.pallas import tpu as pltpu
from jax.sharding import PartitionSpec as P

MESH = pl.DeviceIdType.MESH
CH = 256
UN = 128
NP = 4
PACE = 2
LAT = (3.0, 6.0, 4.0, 6.0, 2.0)
NT = (((1,), (1,)), ((), ()))


def kernel(ny, nx, t_ref, v_ref, m_ref, out_ref, tall, mv, mask, part, crecv, s1, r1, wp, wg,
           ts, tr, cs, cr, as_, ar, zs, zr, gs, gr, is_, ir):
    rows, cols = t_ref.shape
    half = cols // 2
    nj = rows // CH
    nu = rows // UN
    vh = rows // 2
    z = lax.axis_index("row")
    col = lax.axis_index("col")
    x = lax.axis_index("cuts")
    y = lax.div(col, 2)
    h = lax.rem(col, 2)

    def dev(dz=0, dy=0, dx=0, flip=False):
        hh = 1 - h if flip else h
        return (lax.rem(z + dz, 4), 2 * lax.rem(y + dy, ny) + hh, lax.rem(x + dx, nx))

    partners = [dev(dz=d) for d in (1, 2, 3)] + [dev(flip=True)]
    partners += [dev(dy=dy, dx=dx) for dy in range(ny) for dx in range(nx) if dy or dx]
    barrier = pltpu.get_barrier_semaphore()
    for p in partners:
        pl.semaphore_signal(barrier, inc=1, device_id=p, device_id_type=MESH)

    br_, bc_ = m_ref.shape
    e1 = (lax.broadcasted_iota(jnp.int32, (rows, br_), 0) // 64
          == lax.broadcasted_iota(jnp.int32, (rows, br_), 1)).astype(jnp.bfloat16)
    e2 = (lax.broadcasted_iota(jnp.int32, (bc_, cols), 1) // 64
          == lax.broadcasted_iota(jnp.int32, (bc_, cols), 0)).astype(jnp.bfloat16)
    rm = jnp.dot(e1, m_ref[...].astype(jnp.bfloat16), preferred_element_type=jnp.float32).astype(jnp.bfloat16)
    mask[...] = jnp.dot(rm, e2, preferred_element_type=jnp.float32).astype(jnp.bfloat16)
    tall[0] = t_ref[...] * mask[...]
    pl.semaphore_wait(barrier, len(partners))

    def remote(src, dst, ss, rs, to):
        return pltpu.make_async_remote_copy(
            src_ref=src, dst_ref=dst, send_sem=ss, recv_sem=rs, device_id=to, device_id_type=MESH)

    copies = {}
    sent, got = set(), set()

    def start(key, *args):
        copies[key] = remote(*args)
        copies[key].start()

    def wait_send(key):
        if key not in sent:
            sent.add(key)
            copies[key].wait_send()

    def wait_recv(key):
        if key not in got:
            got.add(key)
            copies[key].wait_recv()

    def own(u):
        rs = pl.ds(u * UN, UN)
        if u >= PACE:
            wait_send(("t", 0, u - PACE))
            wait_send(("t", 1, u - PACE))
        start(("t", 0, u), tall.at[0, rs], tall.at[1, rs], ts.at[0, u], tr.at[0, u], dev(dz=1))
        start(("t", 1, u), tall.at[0, rs], tall.at[2, rs], ts.at[1, u], tr.at[1, u], dev(dz=3))

    def fwd(u):
        rs = pl.ds(u * UN, UN)
        for d in (0, 1):
            wait_recv(("t", d, u))
            if u >= PACE:
                wait_send(("t", 2 + d, u - PACE))
        start(("t", 2, u), tall.at[1, rs, pl.ds(0, half)], tall.at[3, rs, pl.ds(0, half)],
              ts.at[2, u], tr.at[2, u], dev(dz=1))
        start(("t", 3, u), tall.at[2, rs, pl.ds(half, half)], tall.at[3, rs, pl.ds(half, half)],
              ts.at[3, u], tr.at[3, u], dev(dz=3))

    def arrived(r, j):
        for u in range(j * CH // UN, (j + 1) * CH // UN):
            for d in {0: (), 1: (0,), 2: (1,), 3: (2, 3)}[r]:
                wait_recv(("t", d, u))

    order = [(0, j) for j in range(nj)] + [(r, j) for j in range(nj) for r in (1, 2)] + [(3, j) for j in range(nj)]
    index = {c: i for i, c in enumerate(order)}

    others = [(dy, dx) for dy in range(ny) for dx in range(nx) if dy or dx]
    k = CH // (ny * nx)
    mine = pl.ds(pl.multiple_of((y * nx + x) * k, k), k)
    done = set()

    def gemm1(q):
        r, j = order[q]
        arrived(r, j)
        p = lax.dot_general(tall[r, j * CH:(j + 1) * CH], mv[...], NT, preferred_element_type=jnp.float32)
        if q >= NP:
            assert q - NP in done
            wait_send(("c", q - NP))
        part[q % NP, 0] = p[:, :vh]
        part[q % NP, 1] = p[:, vh:]
        start(("c", q), part.at[q % NP, 1 - h], crecv.at[q], cs.at[q], cr.at[q], dev(flip=True))

    def scatter(q):
        wait_recv(("c", q))
        full = part[q % NP, h] + crecv[q]
        s1[q] = full.astype(jnp.bfloat16)
        crecv[q] = full
        done.add(q)
        for i, (dy, dx) in enumerate(others):
            p = lax.rem(y + dy, ny) * nx + lax.rem(x + dx, nx)
            remote(s1.at[q, pl.ds(pl.multiple_of(p * k, k), k)], r1.at[q, i], as_.at[q], ar.at[q],
                   dev(dy=dy, dx=dx)).start()
        copies[("a", q)] = remote(r1.at[q], r1.at[q], as_.at[q], ar.at[q], dev(dy=1))

    def finish(q):
        r, j = order[q]
        wait_recv(("a", q))
        total = crecv[q, mine]
        for i in range(len(others)):
            total = total + r1[q, i].astype(jnp.float32)
        w = total.astype(jnp.bfloat16)
        if r == 0:
            wg[q, h, mine] = w
            gather1(q)
        else:
            wp[q] = w
            start(("z", q), wp.at[q], wg.at[q, h, mine], zs.at[q], zr.at[q], dev(dz={1: 3, 2: 1, 3: 2}[r]))

    def gather1(q):
        if order[q][0] != 0:
            wait_recv(("z", q))
        src = wg.at[q, h, mine]
        for dy, dx in others:
            remote(src, src, gs.at[q], gr.at[q], dev(dy=dy, dx=dx)).start()
        copies[("g", q)] = remote(r1.at[q], r1.at[q], gs.at[q], gr.at[q], dev(dy=1))

    def gather2(q):
        wait_recv(("g", q))
        start(("i", q), wg.at[q, h], wg.at[q, h], is_.at[q], ir.at[q], dev(flip=True))

    def gemm2(q):
        r, j = order[q]
        slot = {0: 0, 1: 2, 2: 1, 3: 3}[r]
        for jj in range(nj):
            arrived(slot, jj)
        wait_recv(("i", q))
        w = jnp.concatenate([wg[q, 0], wg[q, 1]], axis=1)
        p = jnp.dot(w, tall[slot], preferred_element_type=jnp.float32)
        js = slice(j * CH, (j + 1) * CH)
        if r == 0:
            out_ref[js] = p
        elif r < 3:
            out_ref[js] = out_ref[js] + p
        else:
            out_ref[js] = (out_ref[js] + p) * mask[js].astype(jnp.float32)

    def prepare():
        mv[...] = v_ref[...] * mask[...]

    events = []

    def at(t, f, *args):
        events.append((t, len(events), f, args))

    unit = 5.1
    for u in range(nu):
        at(max(0.0, unit * (u - 1)), own, u)
        at(unit * nu + 0.5 * unit * (u - 1), fwd, u)
    at(0.1, prepare)
    for q, (r, j) in enumerate(order):
        t = {0: 0.2 + 0.8 * j, 1: 2 * unit * (j + 1) + 2, 2: 2 * unit * (j + 1) + 2.8,
             3: nu * unit + unit * (j + 1) + 4}[r]
        at(t, gemm1, q)
        t += LAT[0]
        at(t, scatter, q)
        t += LAT[1]
        at(t, finish, q)
        if r > 0:
            t += LAT[2]
            at(t, gather1, q)
        t += LAT[3]
        at(t, gather2, q)
        t += LAT[4]
        if r in (1, 2):
            t = max(t, unit * nu + 3)
        at(t, gemm2, q)
    for _, _, f, args in sorted(events, key=lambda e: e[:2]):
        f(*args)
    for key in copies:
        wait_send(key)


def per_device(t_amp, v_int, block_map, ny, nx):
    rows, cols = t_amp.shape
    nq = 4 * rows // CH
    vh = rows // 2
    k = CH // ny // nx
    bf, f32 = jnp.bfloat16, jnp.float32
    dma = pltpu.SemaphoreType.DMA
    vmem = pl.BlockSpec(memory_space=pltpu.VMEM)
    return pl.pallas_call(
        functools.partial(kernel, ny, nx),
        out_shape=jax.ShapeDtypeStruct((rows, cols), f32),
        in_specs=[vmem] * 3,
        out_specs=vmem,
        scratch_shapes=[
            pltpu.VMEM((4, rows, cols), bf),
            pltpu.VMEM((rows, cols), bf),
            pltpu.VMEM((rows, cols), bf),
            pltpu.VMEM((NP, 2, CH, vh), f32),
            pltpu.VMEM((nq, CH, vh), f32),
            pltpu.VMEM((nq, CH, vh), bf),
            pltpu.VMEM((nq, ny * nx - 1, k, vh), bf),
            pltpu.VMEM((nq, k, vh), bf),
            pltpu.VMEM((nq, 2, CH, vh), bf),
            dma((4, rows // UN)), dma((4, rows // UN)),
        ] + [dma((nq,))] * 10,
        compiler_params=pltpu.CompilerParams(
            collective_id=0, has_side_effects=True, vmem_limit_bytes=40 * 2**20),
        cost_estimate=pl.CostEstimate(flops=4 * rows * 4 * rows * cols, bytes_accessed=10 * rows * cols, transcendentals=0),
    )(t_amp, v_int, block_map)


def solution(mesh):
    spec = P("row", ("col", "cuts"))
    body = functools.partial(per_device, ny=mesh.shape["col"] // 2, nx=mesh.shape["cuts"])
    return jax.shard_map(body, mesh=mesh, in_specs=(spec,) * 3, out_specs=spec, check_vma=False)
```

time: 126 us -> 105 us (0.83)
  Pallas kernels: 120 us -> 99.1 us
    pallas_call x1, Pallas kernels: 120 us -> 99.1 us  [per_device(): pl.pallas_call(functools.partial(kernel, ny, nx), out_shape=jax.ShapeDtyp...]
    unnamed x1 -> x7, local copies, waits for them, and re-layouts: 3.97 us -> 5.18 us
where the time goes in v2:
time: 105 us; the launch traced here: 104 us
  Pallas kernels  99.1 us (94%)
  local copies, waits for them, and re-layouts  5.18 us (5%)
    pallas_call x1, Pallas kernels, per_device(): pl.pallas_call(functools.partial(kernel, ny, nx), out_shape=jax.ShapeDtyp...  99.1 us
    unnamed x7, local copies, waits for them, and re-layouts  5.18 us

profile of v2, /device:TPU:1, one launch (start us, length us, event | category | flops | bytes accessed | tf_op | source)
XLA Modules:
  0.0 104.3 jit_solution(15879218313257208500)
XLA Ops:
  0.0 0.0 copy-start
  0.0 1.4 %copy-done = bf16[768,1024]{1,0:T(8,128)(2,1)S(1)} copy-done((bf16[768,1024]{1,0:T(8,128)(2,1)S(1)}, bf16[768,1024]{1,0:T(8,128)(2,1)}, u32[]{:S(2)}) %copy-start) | copy-done | bytes 1572888
  1.4 0.0 copy-start.1
  1.4 1.4 %copy-done.1 = bf16[768,1024]{1,0:T(8,128)(2,1)S(1)} copy-done((bf16[768,1024]{1,0:T(8,128)(2,1)S(1)}, bf16[768,1024]{1,0:T(8,128)(2,1)}, u32[]{:S(2)}) %copy-start.1) | copy-done | bytes 1572888
  2.8 0.0 copy-start.2
  2.8 0.7 copy-done.2
  3.5 99.1 %shard_map.37 = f32[768,1024]{1,0:T(8,128)S(1)} custom-call(bf16[768,1024]{1,0:T(8,128)(2,1)S(1)} %copy-done, bf16[768,1024]{1,0:T(8,128)(2,1)S(1)} %copy-done.1, s32[12,16]{1,0:T(8,128)S(1)} %copy-done.2), custom_call_target="tpu_custom_call" | custom-call | flops 9663676416 | bytes 7864320 | tf_op jit(solution)/shard_map/pallas_call | solution.py:214
  102.7 1.7 %copy.5 = f32[768,1024]{1,0:T(8,128)} copy(f32[768,1024]{1,0:T(8,128)S(1)} %shard_map.37) | data formatting | bytes 6291456
Async XLA Ops:
  0.0 1.4 %copy-start = (bf16[768,1024]{1,0:T(8,128)(2,1)S(1)}, bf16[768,1024]{1,0:T(8,128)(2,1)}, u32[]{:S(2)}) copy-start(bf16[768,1024]{1,0:T(8,128)(2,1)} %t_ref.1) | copy-start | bytes 4718596
  1.4 1.4 %copy-start.1 = (bf16[768,1024]{1,0:T(8,128)(2,1)S(1)}, bf16[768,1024]{1,0:T(8,128)(2,1)}, u32[]{:S(2)}) copy-start(bf16[768,1024]{1,0:T(8,128)(2,1)} %v_ref.1) | copy-start | bytes 4718596
  2.8 0.7 copy-start.2

commit v3 on v2

--- a/solution.py
+++ b/solution.py
@@ -11,8 +11,8 @@
 CH = 256
 UN = 128
 NP = 4
-PACE = 2
-LAT = (3.0, 6.0, 4.0, 6.0, 2.0)
+PACE = 99
+LAT = (4.5, 7.9, 8.1, 17.2, 5.2)
 NT = (((1,), (1,)), ((), ()))
 
 
@@ -175,7 +175,7 @@
     def at(t, f, *args):
         events.append((t, len(events), f, args))
 
-    unit = 5.1
+    unit = 4.1
     for u in range(nu):
         at(max(0.0, unit * (u - 1)), own, u)
         at(unit * nu + 0.5 * unit * (u - 1), fwd, u)

time: 105 us -> 89.5 us (0.85)
  Pallas kernels: 99.1 us -> 84.1 us
    pallas_call x1, Pallas kernels: 99.1 us -> 84.1 us  [per_device(): pl.pallas_call(functools.partial(kernel, ny, nx), out_shape=jax.ShapeDtyp...]
where the time goes in v3:
time: 89.5 us; the launch traced here: 89.3 us
  Pallas kernels  84.1 us (94%)
  local copies, waits for them, and re-layouts  5.18 us (6%)
    pallas_call x1, Pallas kernels, per_device(): pl.pallas_call(functools.partial(kernel, ny, nx), out_shape=jax.ShapeDtyp...  84.1 us
    unnamed x7, local copies, waits for them, and re-layouts  5.18 us

profile of v3, /device:TPU:1, one launch (start us, length us, event | category | flops | bytes accessed | tf_op | source)
XLA Modules:
  0.0 89.3 jit_solution(7354528885208172865)
XLA Ops:
  0.0 0.0 copy-start
  0.0 1.4 %copy-done = bf16[768,1024]{1,0:T(8,128)(2,1)S(1)} copy-done((bf16[768,1024]{1,0:T(8,128)(2,1)S(1)}, bf16[768,1024]{1,0:T(8,128)(2,1)}, u32[]{:S(2)}) %copy-start) | copy-done | bytes 1572888
  1.4 0.0 copy-start.1
  1.4 1.4 %copy-done.1 = bf16[768,1024]{1,0:T(8,128)(2,1)S(1)} copy-done((bf16[768,1024]{1,0:T(8,128)(2,1)S(1)}, bf16[768,1024]{1,0:T(8,128)(2,1)}, u32[]{:S(2)}) %copy-start.1) | copy-done | bytes 1572888
  2.8 0.0 copy-start.2
  2.8 0.7 copy-done.2
  3.5 84.1 %shard_map.37 = f32[768,1024]{1,0:T(8,128)S(1)} custom-call(bf16[768,1024]{1,0:T(8,128)(2,1)S(1)} %copy-done, bf16[768,1024]{1,0:T(8,128)(2,1)S(1)} %copy-done.1, s32[12,16]{1,0:T(8,128)S(1)} %copy-done.2), custom_call_target="tpu_custom_call" | custom-call | flops 9663676416 | bytes 7864320 | tf_op jit(solution)/shard_map/pallas_call | solution.py:214
  87.7 1.7 %copy.5 = f32[768,1024]{1,0:T(8,128)} copy(f32[768,1024]{1,0:T(8,128)S(1)} %shard_map.37) | data formatting | bytes 6291456
Async XLA Ops:
  0.0 1.4 %copy-start = (bf16[768,1024]{1,0:T(8,128)(2,1)S(1)}, bf16[768,1024]{1,0:T(8,128)(2,1)}, u32[]{:S(2)}) copy-start(bf16[768,1024]{1,0:T(8,128)(2,1)} %t_ref.1) | copy-start | bytes 4718596
  1.4 1.4 %copy-start.1 = (bf16[768,1024]{1,0:T(8,128)(2,1)S(1)}, bf16[768,1024]{1,0:T(8,128)(2,1)}, u32[]{:S(2)}) copy-start(bf16[768,1024]{1,0:T(8,128)(2,1)} %v_ref.1) | copy-start | bytes 4718596
  2.8 0.7 copy-start.2

commit v4 on v3

--- a/solution.py
+++ b/solution.py
@@ -11,13 +11,12 @@
 CH = 256
 UN = 128
 NP = 4
-PACE = 99
 LAT = (4.5, 7.9, 8.1, 17.2, 5.2)
 NT = (((1,), (1,)), ((), ()))
 
 
 def kernel(ny, nx, t_ref, v_ref, m_ref, out_ref, tall, mv, mask, part, crecv, s1, r1, wp, wg,
-           ts, tr, cs, cr, as_, ar, zs, zr, gs, gr, is_, ir):
+           ms, ls, ts, tr, cs, cr, as_, ar, zs, zr, gs, gr, is_, ir):
     rows, cols = t_ref.shape
     half = cols // 2
     nj = rows // CH
@@ -39,14 +38,27 @@
     for p in partners:
         pl.semaphore_signal(barrier, inc=1, device_id=p, device_id_type=MESH)
 
-    br_, bc_ = m_ref.shape
-    e1 = (lax.broadcasted_iota(jnp.int32, (rows, br_), 0) // 64
-          == lax.broadcasted_iota(jnp.int32, (rows, br_), 1)).astype(jnp.bfloat16)
-    e2 = (lax.broadcasted_iota(jnp.int32, (bc_, cols), 1) // 64
-          == lax.broadcasted_iota(jnp.int32, (bc_, cols), 0)).astype(jnp.bfloat16)
-    rm = jnp.dot(e1, m_ref[...].astype(jnp.bfloat16), preferred_element_type=jnp.float32).astype(jnp.bfloat16)
-    mask[...] = jnp.dot(rm, e2, preferred_element_type=jnp.float32).astype(jnp.bfloat16)
-    tall[0] = t_ref[...] * mask[...]
+    units = [pl.ds(u * UN, UN) for u in range(nu)]
+    loads = [pltpu.make_async_copy(m_ref, ms, ls.at[0]), pltpu.make_async_copy(v_ref, mv, ls.at[1])]
+    loads += [pltpu.make_async_copy(t_ref.at[rs], tall.at[0, rs], ls.at[2 + u]) for u, rs in enumerate(units)]
+    for c in [loads[0]] + loads[2:] + [loads[1]]:
+        c.start()
+
+    mr, mc = ms.shape
+    e1 = (lax.broadcasted_iota(jnp.int32, (rows, mr), 0) // 64
+          == lax.broadcasted_iota(jnp.int32, (rows, mr), 1)).astype(jnp.bfloat16)
+    e2 = (lax.broadcasted_iota(jnp.int32, (mc, cols), 1) // 64
+          == lax.broadcasted_iota(jnp.int32, (mc, cols), 0)).astype(jnp.bfloat16)
+    loads[0].wait()
+    rm = jnp.dot(e1, ms[...].astype(jnp.bfloat16), preferred_element_type=jnp.float32).astype(jnp.bfloat16)
+
+    def masked(u):
+        rs = units[u]
+        mask[rs] = jnp.dot(rm[u * UN:(u + 1) * UN], e2, preferred_element_type=jnp.float32).astype(jnp.bfloat16)
+        loads[2 + u].wait()
+        tall[0, rs] = tall[0, rs] * mask[rs]
+
+    masked(0)
     pl.semaphore_wait(barrier, len(partners))
 
     def remote(src, dst, ss, rs, to):
@@ -71,19 +83,16 @@
             copies[key].wait_recv()
 
     def own(u):
-        rs = pl.ds(u * UN, UN)
-        if u >= PACE:
-            wait_send(("t", 0, u - PACE))
-            wait_send(("t", 1, u - PACE))
+        rs = units[u]
+        if u > 0:
+            masked(u)
         start(("t", 0, u), tall.at[0, rs], tall.at[1, rs], ts.at[0, u], tr.at[0, u], dev(dz=1))
         start(("t", 1, u), tall.at[0, rs], tall.at[2, rs], ts.at[1, u], tr.at[1, u], dev(dz=3))
 
     def fwd(u):
-        rs = pl.ds(u * UN, UN)
+        rs = units[u]
         for d in (0, 1):
             wait_recv(("t", d, u))
-            if u >= PACE:
-                wait_send(("t", 2 + d, u - PACE))
         start(("t", 2, u), tall.at[1, rs, pl.ds(0, half)], tall.at[3, rs, pl.ds(0, half)],
               ts.at[2, u], tr.at[2, u], dev(dz=1))
         start(("t", 3, u), tall.at[2, rs, pl.ds(half, half)], tall.at[3, rs, pl.ds(half, half)],
@@ -97,7 +106,7 @@
     order = [(0, j) for j in range(nj)] + [(r, j) for j in range(nj) for r in (1, 2)] + [(3, j) for j in range(nj)]
     index = {c: i for i, c in enumerate(order)}
 
-    others = [(dy, dx) for dy in range(ny) for dx in range(nx) if dy or dx]
+    others = [(dy, dx) for dy in (2, 1, 3, 0) for dx in (2, 1, 3, 0) if dy or dx]
     k = CH // (ny * nx)
     mine = pl.ds(pl.multiple_of((y * nx + x) * k, k), k)
     done = set()
@@ -168,7 +177,8 @@
             out_ref[js] = (out_ref[js] + p) * mask[js].astype(jnp.float32)
 
     def prepare():
-        mv[...] = v_ref[...] * mask[...]
+        loads[1].wait()
+        mv[...] = mv[...] * mask[...]
 
     events = []
 
@@ -177,7 +187,7 @@
 
     unit = 4.1
     for u in range(nu):
-        at(max(0.0, unit * (u - 1)), own, u)
+        at(0.0, own, u)
         at(unit * nu + 0.5 * unit * (u - 1), fwd, u)
     at(0.1, prepare)
     for q, (r, j) in enumerate(order):
@@ -214,7 +224,7 @@
     return pl.pallas_call(
         functools.partial(kernel, ny, nx),
         out_shape=jax.ShapeDtypeStruct((rows, cols), f32),
-        in_specs=[vmem] * 3,
+        in_specs=[pl.BlockSpec(memory_space=pltpu.HBM)] * 3,
         out_specs=vmem,
         scratch_shapes=[
             pltpu.VMEM((4, rows, cols), bf),
@@ -226,12 +236,13 @@
             pltpu.VMEM((nq, ny * nx - 1, k, vh), bf),
             pltpu.VMEM((nq, k, vh), bf),
             pltpu.VMEM((nq, 2, CH, vh), bf),
-            dma((4, rows // UN)), dma((4, rows // UN)),
+            pltpu.VMEM(block_map.shape, jnp.int32),
+            dma((2 + rows // UN,)), dma((4, rows // UN)), dma((4, rows // UN)),
         ] + [dma((nq,))] * 10,
         compiler_params=pltpu.CompilerParams(
             collective_id=0, has_side_effects=True, vmem_limit_bytes=40 * 2**20),
         cost_estimate=pl.CostEstimate(flops=4 * rows * 4 * rows * cols, bytes_accessed=10 * rows * cols, transcendentals=0),
-    )(t_amp, v_int, block_map)
+    )(*(pltpu.with_memory_space_constraint(a, pltpu.HBM) for a in (t_amp, v_int, block_map)))
 
 
 def solution(mesh):

time: 89.5 us -> 85.2 us (0.952)
  local copies, waits for them, and re-layouts: 5.18 us -> 1.67 us
    unnamed x7 -> x1, local copies, waits for them, and re-layouts: 5.18 us -> 1.67 us
where the time goes in v4:
time: 85.2 us; the launch traced here: 85.1 us
  Pallas kernels  83.5 us (98%)
  local copies, waits for them, and re-layouts  1.67 us (2%)
    pallas_call x1, Pallas kernels, per_device(): pl.pallas_call(functools.partial(kernel, ny, nx), out_shape=jax.ShapeDtyp...  83.5 us

profile of v4, /device:TPU:1, one launch (start us, length us, event | category | flops | bytes accessed | tf_op | source)
XLA Modules:
  0.0 85.1 jit_solution(14561143694434752778)
XLA Ops:
  0.0 83.5 %shard_map.37 = f32[768,1024]{1,0:T(8,128)S(1)} custom-call(bf16[768,1024]{1,0:T(8,128)(2,1)} %t_ref.1, bf16[768,1024]{1,0:T(8,128)(2,1)} %v_ref.1, s32[12,16]{1,0:T(8,128)} %m_ref.1), custom_call_target="tpu_custom_call" | custom-call | flops 9663676416 | bytes 7864320 | tf_op jit(solution)/shard_map/pallas_call | solution.py:224
  83.5 1.7 %copy.5 = f32[768,1024]{1,0:T(8,128)} copy(f32[768,1024]{1,0:T(8,128)S(1)} %shard_map.37) | data formatting | bytes 6291456

commit v5 on v4

--- a/solution.py
+++ b/solution.py
@@ -11,7 +11,7 @@
 CH = 256
 UN = 128
 NP = 4
-LAT = (4.5, 7.9, 8.1, 17.2, 5.2)
+LAT = (3.6, 7.1, 7.5, 20.9, 6.0)
 NT = (((1,), (1,)), ((), ()))
 
 
@@ -122,8 +122,26 @@
         part[q % NP, 1] = p[:, vh:]
         start(("c", q), part.at[q % NP, 1 - h], crecv.at[q], cs.at[q], cr.at[q], dev(flip=True))
 
+    last = len(order) - 1
+
+    def gemm1_unit(i):
+        r, j = order[last]
+        u = j * CH // UN + i
+        for d in (2, 3):
+            wait_recv(("t", d, u))
+        if i == 0:
+            assert last - NP in done
+            wait_send(("c", last - NP))
+        p = lax.dot_general(tall[r, u * UN:(u + 1) * UN], mv[...], NT, preferred_element_type=jnp.float32)
+        at_ = pl.ds(i * UN, UN)
+        part[last % NP, 0, at_] = p[:, :vh]
+        part[last % NP, 1, at_] = p[:, vh:]
+        start(("c", last + i), part.at[last % NP, 1 - h, at_], crecv.at[last, at_], cs.at[last + i],
+              cr.at[last + i], dev(flip=True))
+
     def scatter(q):
-        wait_recv(("c", q))
+        for i in range(CH // UN if q == last else 1):
+            wait_recv(("c", q + i))
         full = part[q % NP, h] + crecv[q]
         s1[q] = full.astype(jnp.bfloat16)
         crecv[q] = full
@@ -176,6 +194,17 @@
         else:
             out_ref[js] = (out_ref[js] + p) * mask[js].astype(jnp.float32)
 
+    def gemm2_part(own_half):
+        r, j = order[last]
+        js = slice(j * CH, (j + 1) * CH)
+        side = h if own_half else 1 - h
+        if not own_half:
+            wait_recv(("i", last))
+        p = jnp.dot(wg[last, side], tall[r, pl.ds(pl.multiple_of(side * vh, vh), vh)],
+                    preferred_element_type=jnp.float32)
+        total = out_ref[js] + p
+        out_ref[js] = total if own_half else total * mask[js].astype(jnp.float32)
+
     def prepare():
         loads[1].wait()
         mv[...] = mv[...] * mask[...]
@@ -185,7 +214,7 @@
     def at(t, f, *args):
         events.append((t, len(events), f, args))
 
-    unit = 4.1
+    unit = 3.9
     for u in range(nu):
         at(0.0, own, u)
         at(unit * nu + 0.5 * unit * (u - 1), fwd, u)
@@ -193,7 +222,11 @@
     for q, (r, j) in enumerate(order):
         t = {0: 0.2 + 0.8 * j, 1: 2 * unit * (j + 1) + 2, 2: 2 * unit * (j + 1) + 2.8,
              3: nu * unit + unit * (j + 1) + 4}[r]
-        at(t, gemm1, q)
+        if q == last:
+            at(t, gemm1_unit, 0)
+            at(t, gemm1_unit, 1)
+        else:
+            at(t, gemm1, q)
         t += LAT[0]
         at(t, scatter, q)
         t += LAT[1]
@@ -203,10 +236,15 @@
             at(t, gather1, q)
         t += LAT[3]
         at(t, gather2, q)
+        if q == last:
+            at(t, gemm2_part, True)
         t += LAT[4]
         if r in (1, 2):
             t = max(t, unit * nu + 3)
-        at(t, gemm2, q)
+        if q == last:
+            at(t, gemm2_part, False)
+        else:
+            at(t, gemm2, q)
     for _, _, f, args in sorted(events, key=lambda e: e[:2]):
         f(*args)
     for key in copies:
@@ -238,7 +276,7 @@
             pltpu.VMEM((nq, 2, CH, vh), bf),
             pltpu.VMEM(block_map.shape, jnp.int32),
             dma((2 + rows // UN,)), dma((4, rows // UN)), dma((4, rows // UN)),
-        ] + [dma((nq,))] * 10,
+        ] + [dma((nq + CH // UN - 1,))] * 2 + [dma((nq,))] * 8,
         compiler_params=pltpu.CompilerParams(
             collective_id=0, has_side_effects=True, vmem_limit_bytes=40 * 2**20),
         cost_estimate=pl.CostEstimate(flops=4 * rows * 4 * rows * cols, bytes_accessed=10 * rows * cols, transcendentals=0),

time: 85.2 us -> 84.3 us (0.989)
  Pallas kernels: 83.5 us -> 82.5 us
    pallas_call x1, Pallas kernels: 83.5 us -> 82.5 us  [per_device(): pl.pallas_call(functools.partial(kernel, ny, nx), out_shape=jax.ShapeDtyp...]
where the time goes in v5:
time: 84.3 us; the launch traced here: 84.2 us
  Pallas kernels  82.5 us (98%)
  local copies, waits for them, and re-layouts  1.67 us (2%)
    pallas_call x1, Pallas kernels, per_device(): pl.pallas_call(functools.partial(kernel, ny, nx), out_shape=jax.ShapeDtyp...  82.5 us

profile of v5, /device:TPU:1, one launch (start us, length us, event | category | flops | bytes accessed | tf_op | source)
XLA Modules:
  0.0 84.2 jit_solution(1696110488513029577)
XLA Ops:
  0.0 82.5 %shard_map.37 = f32[768,1024]{1,0:T(8,128)S(1)} custom-call(bf16[768,1024]{1,0:T(8,128)(2,1)} %t_ref.1, bf16[768,1024]{1,0:T(8,128)(2,1)} %v_ref.1, s32[12,16]{1,0:T(8,128)} %m_ref.1), custom_call_target="tpu_custom_call" | custom-call | flops 9663676416 | bytes 7864320 | tf_op jit(solution)/shard_map/pallas_call | solution.py:262
  82.5 1.7 %copy.5 = f32[768,1024]{1,0:T(8,128)} copy(f32[768,1024]{1,0:T(8,128)S(1)} %shard_map.37) | data formatting | bytes 6291456

commit v6 on v5

--- a/solution.py
+++ b/solution.py
@@ -106,7 +106,7 @@
     order = [(0, j) for j in range(nj)] + [(r, j) for j in range(nj) for r in (1, 2)] + [(3, j) for j in range(nj)]
     index = {c: i for i, c in enumerate(order)}
 
-    others = [(dy, dx) for dy in (2, 1, 3, 0) for dx in (2, 1, 3, 0) if dy or dx]
+    others = [(dy, dx) for dy in (0, 1, 3, 2) for dx in (0, 1, 3, 2) if dy or dx]
     k = CH // (ny * nx)
     mine = pl.ds(pl.multiple_of((y * nx + x) * k, k), k)
     done = set()
@@ -205,6 +205,11 @@
         total = out_ref[js] + p
         out_ref[js] = total if own_half else total * mask[js].astype(jnp.float32)
 
+    def drain(q):
+        for key in list(copies):
+            if key[0] == "t" or key[1] <= q:
+                wait_send(key)
+
     def prepare():
         loads[1].wait()
         mv[...] = mv[...] * mask[...]
@@ -229,10 +234,14 @@
             at(t, gemm1, q)
         t += LAT[0]
         at(t, scatter, q)
+        if q == last:
+            at(t, drain, last - 3)
         t += LAT[1]
         at(t, finish, q)
         if r > 0:
             t += LAT[2]
+            if q == last:
+                at(t, drain, last - 2)
             at(t, gather1, q)
         t += LAT[3]
         at(t, gather2, q)
@@ -242,6 +251,7 @@
         if r in (1, 2):
             t = max(t, unit * nu + 3)
         if q == last:
+            at(t, drain, last - 1)
             at(t, gemm2_part, False)
         else:
             at(t, gemm2, q)

time: 84.3 us -> 85.2 us (1.011)
  Pallas kernels: 82.5 us -> 83.4 us
    pallas_call x1, Pallas kernels: 82.5 us -> 83.4 us  [per_device(): pl.pallas_call(functools.partial(kernel, ny, nx), out_shape=jax.ShapeDtyp...]
where the time goes in v6:
time: 85.2 us; the launch traced here: 85.1 us
  Pallas kernels  83.4 us (98%)
  local copies, waits for them, and re-layouts  1.67 us (2%)
    pallas_call x1, Pallas kernels, per_device(): pl.pallas_call(functools.partial(kernel, ny, nx), out_shape=jax.ShapeDtyp...  83.4 us

profile of v6, /device:TPU:1, one launch (start us, length us, event | category | flops | bytes accessed | tf_op | source)
XLA Modules:
  0.0 85.1 jit_solution(7461946378519975805)
XLA Ops:
  0.0 83.4 %shard_map.37 = f32[768,1024]{1,0:T(8,128)S(1)} custom-call(bf16[768,1024]{1,0:T(8,128)(2,1)} %t_ref.1, bf16[768,1024]{1,0:T(8,128)(2,1)} %v_ref.1, s32[12,16]{1,0:T(8,128)} %m_ref.1), custom_call_target="tpu_custom_call" | custom-call | flops 9663676416 | bytes 7864320 | tf_op jit(solution)/shard_map/pallas_call | solution.py:272
  83.4 1.7 %copy.5 = f32[768,1024]{1,0:T(8,128)} copy(f32[768,1024]{1,0:T(8,128)S(1)} %shard_map.37) | data formatting | bytes 6291456

commit v7 on v6

--- a/solution.py
+++ b/solution.py
@@ -106,7 +106,7 @@
     order = [(0, j) for j in range(nj)] + [(r, j) for j in range(nj) for r in (1, 2)] + [(3, j) for j in range(nj)]
     index = {c: i for i, c in enumerate(order)}
 
-    others = [(dy, dx) for dy in (0, 1, 3, 2) for dx in (0, 1, 3, 2) if dy or dx]
+    others = [(dy, dx) for dy in (2, 1, 3, 0) for dx in (2, 1, 3, 0) if dy or dx]
     k = CH // (ny * nx)
     mine = pl.ds(pl.multiple_of((y * nx + x) * k, k), k)
     done = set()
@@ -222,7 +222,7 @@
     unit = 3.9
     for u in range(nu):
         at(0.0, own, u)
-        at(unit * nu + 0.5 * unit * (u - 1), fwd, u)
+        at(24.0 + 0.5 * unit * u, fwd, u)
     at(0.1, prepare)
     for q, (r, j) in enumerate(order):
         t = {0: 0.2 + 0.8 * j, 1: 2 * unit * (j + 1) + 2, 2: 2 * unit * (j + 1) + 2.8,

time: 85.2 us -> 84.2 us (0.988)
  Pallas kernels: 83.4 us -> 82.4 us
    pallas_call x1, Pallas kernels: 83.4 us -> 82.4 us  [per_device(): pl.pallas_call(functools.partial(kernel, ny, nx), out_shape=jax.ShapeDtyp...]
where the time goes in v7:
time: 84.2 us; the launch traced here: 84.1 us
  Pallas kernels  82.4 us (98%)
  local copies, waits for them, and re-layouts  1.67 us (2%)
    pallas_call x1, Pallas kernels, per_device(): pl.pallas_call(functools.partial(kernel, ny, nx), out_shape=jax.ShapeDtyp...  82.4 us

profile of v7, /device:TPU:1, one launch (start us, length us, event | category | flops | bytes accessed | tf_op | source)
XLA Modules:
  0.0 84.1 jit_solution(6863930946465468453)
XLA Ops:
  0.0 82.4 %shard_map.37 = f32[768,1024]{1,0:T(8,128)S(1)} custom-call(bf16[768,1024]{1,0:T(8,128)(2,1)} %t_ref.1, bf16[768,1024]{1,0:T(8,128)(2,1)} %v_ref.1, s32[12,16]{1,0:T(8,128)} %m_ref.1), custom_call_target="tpu_custom_call" | custom-call | flops 9663676416 | bytes 7864320 | tf_op jit(solution)/shard_map/pallas_call | solution.py:272
  82.4 1.7 %copy.5 = f32[768,1024]{1,0:T(8,128)} copy(f32[768,1024]{1,0:T(8,128)S(1)} %shard_map.37) | data formatting | bytes 6291456
